TPU v7x, 256 devices: a whole 4x4x8 slice. The times are simulated.
256 devices in a mesh: dp: 32 (over z_hi, x, core), tensor: 8 (over z_lo, y).
Axes of the slice: x: 4, y: 4, z: 8 (z_hi: 4, z_lo: 2; z = z_hi * 2 + z_lo), core: 2. Of those that a mesh axis runs over, the one named last changes fastest.
Arguments:
- hidden: bfloat16 [16384, 16384], P('dp')
- head: bfloat16 [2048, 16384], P('tensor', 'dp')
- targets: int32 [16384], P('dp'), may hold values from 0 to 127999, as said below
- block_index: int32 [2], replicated, may hold values from 0 to 124, as said below
- lse_rest: float32 [16384], P('dp'), may hold values from 6 to 12
- cotangent: float32 [16384], P('dp'), may hold values from 0.5 to 1.5
Outputs:
- loss: float32 [16384], P('dp')
- head_grad: float32 [2048, 16384], P('tensor', 'dp')
Inputs may be any that keep to these rules, and one draw needn't show every extreme that they name: `block_index`: distinct block numbers of the vocabulary. Every target lies in one of the window's blocks: targets // 1024 is an entry of block_index.
All inputs are finite; a program needn't handle non-finite values.
Results may differ from a plain program's by a relative error of at most 0.003.
Values may be sent and summed in bfloat16 or wider, within the bound.
No kernel may reach another device: no remote copies, remote signals or barrier semaphores. Data moves between devices by JAX's collectives and lax.ppermute only.
A program may use at most 128 MiB of HBM per device.

v0:
```python
import jax
import jax.numpy as jnp
from jax import lax
from jax.sharding import PartitionSpec as P

BLOCK = 1024


z_weight = 0.0001


def shards(hidden, head, targets, block_index, lse_rest, cotangent):
    vocab_rows = head.shape[0]
    first_row = lax.axis_index("tensor") * vocab_rows
    row_ids = first_row + lax.iota(jnp.int32, vocab_rows)
    block_of = row_ids // BLOCK
    block_match = (block_of[:, None] == lax.iota(jnp.int32, block_index.shape[0])[None, :]).astype(
        jnp.int32
    )
    vocab_ids = jnp.sum(block_match * block_index[None, :], axis=1) * BLOCK + row_ids % BLOCK
    columns = hidden
    logits = lax.dot_general(
        columns,
        lax.all_gather(head, "dp", axis=1, tiled=True),
        (((1,), (1,)), ((), ())),
        preferred_element_type=jnp.float32,
    )
    target_hit = vocab_ids[None, :] == targets[:, None]
    target_pick = jnp.sum(jnp.where(target_hit, logits, jnp.float32(0.0)), axis=1)
    local_max = jnp.max(logits, axis=1)
    row_max = lax.pmax(local_max, "tensor")
    row_total, target_logit = lax.psum(
        (jnp.sum(jnp.exp(logits - row_max[:, None]), axis=1), target_pick), "tensor"
    )
    lse_window = row_max + jnp.log(row_total)
    larger = jnp.maximum(lse_window, lse_rest)
    log_total = larger + jnp.log(jnp.exp(lse_window - larger) + jnp.exp(lse_rest - larger))
    loss = log_total - target_logit + z_weight * log_total * log_total
    softmax = jnp.exp(logits - log_total[:, None])
    grad_logits = (
        cotangent[:, None]
        * (softmax * (1.0 + 2.0 * z_weight * log_total)[:, None] - target_hit.astype(jnp.float32))
    ).astype(jnp.bfloat16)
    columns = hidden
    shares = lax.psum_scatter(
        lax.dot_general(
            columns, grad_logits, (((0,), (0,)), ((), ())), preferred_element_type=jnp.float32
        ),
        "dp",
        scatter_dimension=0,
        tiled=True,
    )
    head_grad = jnp.transpose(shares)
    return (loss, head_grad)


def solution(mesh):
    placed = (P("dp", None), P("tensor", "dp"), P("dp"), P(), P("dp"), P("dp"))
    return jax.shard_map(
        shards, mesh=mesh, in_specs=placed, out_specs=(P("dp"), P("tensor", "dp")), check_vma=False
    )
```

profile of v0, /device:TPU:8, one launch (start us, length us, event | category | flops | bytes accessed | tf_op | source)
XLA Modules:
  0.0 330.3 jit_solution(13372195436807537665)
XLA Ops:
  7.2 0.0 all-gather.2.cloned.1.call-start
  7.2 0.7 all-gather.2.cloned.1.call-update
  7.9 0.0 reduce-scatter.2.cloned.1.call-start
  8.0 0.7 fusion.11
  8.7 0.0 copy-start
  8.7 0.0 copy-start.2
  8.7 0.0 copy-start.1
  8.7 90.0 %all-gather.2.cloned.1.call-done = bf16[256,16384]{1,0:T(8,128)(2,1)} async-done(((bf16[256,512]{1,0:T(8,128)(2,1)}), bf16[256,16384]{1,0:T(8,128)(2,1)}) %all-gather.2.cloned.1.call-update) | async-done | bytes 8388624 | tf_op jit(solution)/shard_map/all_gather | solution.py:24
  98.7 10.6 %fusion.15 = (f32[512]{0:T(512)S(1)}, f32[512,256]{0,1:T(8,128)S(1)}) fusion(bf16[512,16384]{1,0:T(8,128)(2,1)} %param.6, bf16[256,16384]{1,0:T(8,128)(2,1)} %all-gather.2.cloned.1.call-done), kind=kOutput, calls=%fused_computation.30 | convolution fusion | flops 4295097856 | bytes 25692160 | tf_op jit(solution)/shard_map/dot_general | solution.py:22
  109.3 16.8 %pmax.7 = f32[512]{0:T(512)S(1)} all-reduce(f32[512]{0:T(512)S(1)} %get-tuple-element.8), channel_id=1, replica_groups=mesh['dp'=32,'tensor'=8] {'tensor'}, use_global_device_ids=true, to_apply=%region_1.2 | all-reduce | flops 512 | bytes 4096 | tf_op jit(solution)/shard_map/pmax | solution.py:31
  126.1 0.0 copy-done
  126.1 0.1 fusion
  126.2 17.2 %all-reduce = (f32[512]{0:T(512)S(1)}, f32[512]{0:T(512)S(1)}) all-reduce(f32[512]{0:T(512)S(1)} %get-tuple-element.3, f32[512]{0:T(512)S(1)} %get-tuple-element.2), channel_id=1, replica_groups=mesh['dp'=32,'tensor'=8] {'tensor'}, use_global_device_ids=true, to_apply=%region_3.4 | all-reduce | flops 1024 | bytes 8192 | tf_op jit(solution)/shard_map/psum | solution.py:32
  143.4 0.0 copy-done.2
  143.4 0.0 copy-done.1
  143.4 13.9 %convolution_bitcast_fusion = f32[16384,256]{0,1:T(8,128)} fusion(bf16[512,16384]{1,0:T(8,128)(2,1)} %param.6, f32[512,256]{0,1:T(8,128)S(1)} %get-tuple-element.9, f32[512]{0:T(512)S(1)} %get-tuple-element.6, f32[512]{0:T(512)S(1)} %get-tuple-element.7, f32[512]{0:T(512)S(1)} %copy-done.1, s32[512]{0:T(512)S(1)} %copy-done, s32[256]{0:T(256)S(1)} %fusion.13), kind=kOutput, calls=%fused_computation | convolution fusion | flops 4295884800 | bytes 34087936 | tf_op jit(solution)/shard_map/dot_general | solution.py:46
  157.3 0.0 reduce-scatter.2.cloned.1.call-update
  157.4 0.6 fusion.10
  158.0 165.5 %reduce-scatter.2.cloned.1.call-done = f32[512,256]{0,1:T(8,128)} async-done(((f32[16384,256]{0,1:T(8,128)}), f32[512,256]{0,1:T(8,128)}) %reduce-scatter.2.cloned.1.call-update) | async-done | bytes 524304 | tf_op jit(solution)/shard_map/reduce_scatter | solution.py:45
  (3 shorter events, 0.0 us)
Async XLA Ops:
  7.2 91.5 %all-gather.2.cloned.1.call-start = ((), (), s32[]{:S(2)}) async-start(), calls=%async_computation.1 | async-start | bytes 8650752 | tf_op jit(solution)/shard_map/all_gather | solution.py:24
  7.9 315.6 %reduce-scatter.2.cloned.1.call-start = ((), (), s32[]{:S(2)}) async-start(), calls=%async_computation.2 | async-start | bytes 17301504 | tf_op jit(solution)/shard_map/reduce_scatter | solution.py:45
  8.7 117.4 %copy-start = (s32[512]{0:T(512)S(1)}, s32[512]{0:T(512)}, u32[]{:S(2)}) copy-start(s32[512]{0:T(512)} %param.8) | copy-start | bytes 6148
  8.7 134.7 %copy-start.2 = (f32[512]{0:T(512)S(1)}, f32[512]{0:T(512)}, u32[]{:S(2)}) copy-start(f32[512]{0:T(512)} %param.10) | copy-start | bytes 6148
  8.7 134.7 %copy-start.1 = (f32[512]{0:T(512)S(1)}, f32[512]{0:T(512)}, u32[]{:S(2)}) copy-start(f32[512]{0:T(512)} %param.11) | copy-start | bytes 6148
Sparse Core Ops, SparseCore 0:
  10.5 88.1 all-gather.1
  157.5 165.9 reduce-scatter.1
where the time goes:
time: 331 us; the launch traced here: 330 us
  waiting for transfers between devices  256 us (77%)
  blocking collectives  33.9 us (10%)
  matrix products  24.5 us (7%)
  between operations  14.1 us (4%)
    reduce_scatter x1, waiting for transfers between devices, shards(): lax.psum_scatter(lax.dot_general(columns, grad_logits, (((0,), (0,)), (()...  166 us
    all_gather x1, waiting for transfers between devices, shards(): lax.all_gather(head, 'dp', axis=1, tiled=True)  90 us
    psum x1, blocking collectives, shards(): lax.psum((jnp.sum(jnp.exp(logits - row_max[:, None]), axis=1), target_pic...  17.2 us
    pmax x1, blocking collectives, shards(): row_max = lax.pmax(local_max, 'tensor')  16.8 us
    dot_general x1, matrix products, shards(): lax.dot_general(columns, grad_logits, (((0,), (0,)), ((), ())), preferred...  13.9 us
    dot_general x1, matrix products, shards(): lax.dot_general(columns, lax.all_gather(head, 'dp', axis=1, tiled=True),...  10.6 us
  transfers between devices with their start and end apart: 2, of which 2 were waited for; matrix products, arithmetic and copies ran while one was open for 0% of the time, Pallas kernels for 0%

commit v1 on v0

v1 whole, which is shorter than its diff:
```python
import jax
import jax.numpy as jnp
from jax import lax
from jax.experimental import pallas as pl
from jax.experimental.pallas import tpu as pltpu
from jax.sharding import Mesh
from jax.sharding import PartitionSpec as P

BLOCK = 1024
z_weight = 0.0001

AXES = ("zh", "x", "c", "zl", "y")
SIZES = (4, 4, 2, 2, 4)
DP = ("zh", "x", "c")
TENSOR = ("zl", "y")

ROWS = 256
TOK = 512
WIDE = 512
PR, QR = 192, 64

F32 = jnp.float32
BF16 = jnp.bfloat16
MIB = 1024 * 1024


def move(value, axis, by):
    n = SIZES[AXES.index(axis)]
    return lax.ppermute(value, axis, [(i, (i + by) % n) for i in range(n)])


def params(mib):
    return pltpu.CompilerParams(vmem_limit_bytes=mib * MIB)


def whole(shape):
    return pl.BlockSpec(shape, lambda: (0,) * len(shape))


def local_call(body, outs, *args):
    size = sum(a.size * a.dtype.itemsize for a in args) + sum(
        o.size * o.dtype.itemsize for o in outs
    )
    return pl.pallas_call(
        body,
        out_shape=outs,
        in_specs=[whole(a.shape) for a in args],
        out_specs=[whole(o.shape) for o in outs],
        compiler_params=params(16),
        cost_estimate=pl.CostEstimate(flops=0, bytes_accessed=size, transcendentals=0),
    )(*args)


def pick(hidden, at):
    n = at.shape[0]

    def body(at_ref, h_ref, o_ref, arrived):
        copies = [
            pltpu.make_async_copy(
                h_ref.at[:, pl.ds(pl.multiple_of(at_ref[k] * WIDE, WIDE), WIDE)],
                o_ref.at[k],
                arrived.at[k],
            )
            for k in range(n)
        ]
        for copy in copies:
            copy.start()
        for copy in copies:
            copy.wait()

    return pl.pallas_call(
        body,
        out_shape=jax.ShapeDtypeStruct((n, TOK, WIDE), BF16),
        in_specs=[
            pl.BlockSpec(memory_space=pltpu.SMEM),
            pl.BlockSpec(memory_space=pl.ANY),
        ],
        out_specs=pl.BlockSpec(memory_space=pltpu.VMEM),
        scratch_shapes=[pltpu.SemaphoreType.DMA((n,))],
        compiler_params=params(50),
        cost_estimate=pl.CostEstimate(
            flops=0, bytes_accessed=6 * n * TOK * WIDE * 2, transcendentals=0
        ),
    )(at, hidden)


def block_call(compute, plan, outs, mine, theirs, others, rows):
    n = len(plan)

    def body(m_ref, t0_ref, t1_ref, *refs):
        t_refs = (t0_ref, t1_ref)
        hold, arrived = refs[-2:]
        copies = [
            pltpu.make_async_copy(ref, hold.at[i, side], arrived.at[i, side])
            for i, (slot, _) in enumerate(plan)
            for side, ref in enumerate((m_ref.at[slot], t_refs[slot // 8].at[slot % 8]))
        ]
        for copy in copies:
            copy.start()
        for i, (_, parts) in enumerate(plan):
            copies[2 * i].wait()
            copies[2 * i + 1].wait()
            compute(i, parts, hold, refs[: len(others)], refs[len(others) : -2])

    return pl.pallas_call(
        body,
        out_shape=outs,
        in_specs=[pl.BlockSpec(memory_space=pl.ANY)] * 3 + [whole(o.shape) for o in others],
        out_specs=[whole(o.shape) for o in outs],
        scratch_shapes=[
            pltpu.VMEM((n, 2, TOK, WIDE), BF16),
            pltpu.SemaphoreType.DMA((n, 2)),
        ],
        compiler_params=params(50),
        cost_estimate=pl.CostEstimate(
            flops=4 * rows * WIDE * TOK,
            bytes_accessed=2 * n * TOK * WIDE * 2,
            transcendentals=0,
        ),
    )(mine, *theirs, *others)


def add_logits(total, plan, pieces, mine, theirs):
    has_total = total is not None

    def compute(i, parts, hold, refs, outs):
        (out,) = outs
        if i == 0:
            out[...] = refs[-1][...] if has_total else jnp.zeros_like(out)
        for piece, start, rows, to in parts:
            a = refs[piece][start : start + rows, :]
            for side in range(2):
                out[to : to + rows, side * TOK : (side + 1) * TOK] += lax.dot_general(
                    a, hold[i, side], (((1,), (1,)), ((), ())), preferred_element_type=F32
                )

    return block_call(
        compute,
        plan,
        [jax.ShapeDtypeStruct((ROWS, 2 * TOK), F32)],
        mine,
        theirs,
        list(pieces) + ([total] if has_total else []),
        sum(r for _, parts in plan for _, _, r, _ in parts),
    )[0]


def gradient_terms(plan, outs, grad, mine, theirs):
    def compute(i, parts, hold, refs, outs):
        (g_ref,) = refs
        term = jnp.dot(
            g_ref[:, :TOK], hold[i, 0], preferred_element_type=F32
        ) + jnp.dot(g_ref[:, TOK:], hold[i, 1], preferred_element_type=F32)
        for out, to, start, rows in parts:
            outs[out][to : to + rows, :] = term[start : start + rows, :].astype(
                outs[out].dtype
            )

    return block_call(compute, plan, outs, mine, theirs, [grad], len(plan) * ROWS)


def statistics(partial, other, hit):
    def body(mine, theirs, hit_ref, logits, stats):
        total = mine[...] + jnp.concatenate([theirs[:, TOK:], theirs[:, :TOK]], axis=1)
        logits[...] = total
        top = jnp.max(total, axis=0, keepdims=True)
        stats[0:1, :] = top
        stats[1:2, :] = jnp.sum(jnp.exp(total - top), axis=0, keepdims=True)
        stats[2:3, :] = jnp.sum(total * hit_ref[...], axis=0, keepdims=True)

    outs = [
        jax.ShapeDtypeStruct((ROWS, 2 * TOK), F32),
        jax.ShapeDtypeStruct((3, 2 * TOK), F32),
    ]
    return local_call(body, outs, partial, other, hit)


def gradient(logits, hit, stats, lse_rest, cotangent):
    def body(logits_ref, hit_ref, s, rest, cot, loss, grad):
        top = s[0]
        row_max = jnp.max(top, axis=0, keepdims=True)
        row_total = jnp.sum(s[1] * jnp.exp(top - row_max), axis=0, keepdims=True)
        target_logit = jnp.sum(s[2], axis=0, keepdims=True)
        lse_window = row_max + jnp.log(row_total)
        larger = jnp.maximum(lse_window, rest[...])
        log_total = larger + jnp.log(
            jnp.exp(lse_window - larger) + jnp.exp(rest[...] - larger)
        )
        loss[...] = log_total - target_logit + z_weight * log_total * log_total
        softmax = jnp.exp(logits_ref[...] - log_total)
        grad[...] = (
            cot[...] * (softmax * (1.0 + 2.0 * z_weight * log_total) - hit_ref[...])
        ).astype(BF16)

    outs = [
        jax.ShapeDtypeStruct((1, 2 * TOK), F32),
        jax.ShapeDtypeStruct((ROWS, 2 * TOK), BF16),
    ]
    return local_call(body, outs, logits, hit, stats, lse_rest, cotangent)


def gathered_logits(head, hidden, at, sibling_at):
    zb, za, zf = (move(head[:PR], "zh", by) for by in (1, -1, 2))
    xb, xa, xf = (move(head, "x", by) for by in (1, -1, 2))
    part = move(pick(hidden, sibling_at[:8]), "c", 1)
    zb, rest_at = lax.optimization_barrier((zb, sibling_at[8:]))
    theirs = (part, move(pick(hidden, rest_at), "c", 1))
    mine = pick(hidden, at)
    p = jnp.concatenate([za, zb, zf], axis=0)
    q = jnp.concatenate([head[PR:], xa[PR:], xb[PR:], xf[PR:]], axis=0)
    pb, pa, pf = (move(p, "x", by) for by in (1, -1, 2))
    qb, qa, qf = (move(q, "zh", by) for by in (1, -1, 2))

    first = [
        (0, [(0, 0, ROWS, 0)]),
        (1, [(1, 0, ROWS, 0)]),
        (3, [(2, 0, ROWS, 0)]),
        (2, [(3, 0, ROWS, 0)]),
        (4, [(4, 0, PR, 0)]),
        (12, [(5, 0, PR, 0)]),
        (8, [(6, 0, PR, 0)]),
    ]
    total = add_logits(None, first, [head, xa, xb, xf, za, zb, zf], mine, theirs)
    second = {slot: [] for slot in range(16)}
    third = {slot: [] for slot in range(16)}
    for k, dz in enumerate((1, 3, 2)):
        second[dz * 4 + 1].append((0, k * PR, PR, 0))
        second[dz * 4 + 3].append((1, k * PR, PR, 0))
        third[dz * 4 + 2].append((0, k * PR, PR, 0))
    for k, dx in enumerate((0, 1, 3, 2)):
        second[4 + dx].append((2, k * QR, QR, PR))
        second[12 + dx].append((3, k * QR, QR, PR))
        third[8 + dx].append((1, k * QR, QR, PR))
    second = [(slot, parts) for slot, parts in second.items() if parts]
    third = [(slot, parts) for slot, parts in third.items() if parts]
    total = add_logits(total, second, [pa, pb, qa, qb], mine, theirs)
    return add_logits(total, third, [pf, qf], mine, theirs), mine, theirs


def scattered_gradient(grad, mine, theirs):
    def array(rows, dtype):
        return jax.ShapeDtypeStruct((rows, WIDE), dtype)

    outs = [array(3 * PR, BF16)] * 3 + [array(3 * PR, F32)] + [array(4 * QR, BF16)] * 3
    plan = []
    for dz in (1, 2, 3):
        for dx in (1, 2, 3, 0):
            p_out = 3 if dx == 0 else dx - 1
            plan.append(
                (dz * 4 + dx, [(p_out, (dz - 1) * PR, 0, PR), (3 + dz, dx * QR, PR, QR)])
            )
    p1, p2, p3, p_here, q1, q2, q3 = gradient_terms(plan, outs, grad, mine, theirs)
    p1, p2, p3 = move(p1, "x", 1), move(p2, "x", 2), move(p3, "x", -1)
    q1, q2, q3 = move(q1, "zh", 1), move(q2, "zh", 2), move(q3, "zh", -1)
    outs = [array(4 * PR, F32), array(4 * QR, F32)]
    plan = [(dx, [(0, dx * PR, 0, PR), (1, dx * QR, PR, QR)]) for dx in range(4)]
    own, q_here = gradient_terms(plan, outs, grad, mine, theirs)

    def settle(kept, one, two, three, k, rows):
        at = pl.ds(k * rows, rows)
        return kept[at, :] + (
            one[at, :].astype(F32) + two[at, :].astype(F32) + three[at, :].astype(F32)
        )

    def p_body(kept, one, two, three, *outs):
        for k in range(3):
            outs[k][...] = settle(kept, one, two, three, k, PR).astype(BF16)

    z1, z2, z3 = local_call(p_body, [array(PR, BF16)] * 3, p_here, p1, p2, p3)
    z1, z2, z3 = move(z1, "zh", 1), move(z2, "zh", 2), move(z3, "zh", -1)

    def q_body(own, kept, one, two, three, *outs):
        for dx in range(4):
            out = outs[dx]
            out[:PR, :] = own[dx * PR : (dx + 1) * PR, :].astype(out.dtype)
            out[PR:, :] = settle(kept, one, two, three, dx, QR).astype(out.dtype)

    x_here, x1, x2, x3 = local_call(
        q_body, [array(ROWS, F32)] + [array(ROWS, BF16)] * 3, own, q_here, q1, q2, q3
    )
    x1, x2, x3 = move(x1, "x", 1), move(x2, "x", 2), move(x3, "x", -1)

    def last_body(here, x1, x2, x3, z1, z2, z3, out):
        out[...] = settle(here, x1, x2, x3, 0, ROWS)
        out[:PR, :] += z1[...].astype(F32) + z2[...].astype(F32) + z3[...].astype(F32)

    (out,) = local_call(last_body, [array(ROWS, F32)], x_here, x1, x2, x3, z1, z2, z3)
    return out


def shards(hidden, head, targets, block_index, lse_rest, cotangent):
    zh, x, c = (lax.axis_index(a) for a in DP)
    first_row = lax.axis_index(TENSOR) * ROWS
    row_ids = first_row + lax.iota(jnp.int32, ROWS)
    block_of = row_ids // BLOCK
    block_match = (block_of[:, None] == lax.iota(jnp.int32, block_index.shape[0])[None, :]).astype(
        jnp.int32
    )
    vocab_ids = jnp.sum(block_match * block_index[None, :], axis=1) * BLOCK + row_ids % BLOCK

    k = lax.iota(jnp.int32, 16)
    at = (((zh + k // 4) % 4) * 4 + (x + k % 4) % 4) * 2
    at, sibling_at = at + c, at + (1 - c)

    facts = jnp.stack([targets.astype(F32), lse_rest, cotangent])
    facts = jnp.concatenate([facts, move(facts, "c", 1)], axis=1)
    hit = (vocab_ids[:, None] == facts[0].astype(jnp.int32)[None, :]).astype(F32)

    partial, mine, theirs = gathered_logits(head, hidden, at, sibling_at)
    logits, stats = statistics(partial, move(partial, "c", 1), hit)
    stats = lax.all_to_all(
        jnp.broadcast_to(stats[None], (8,) + stats.shape), TENSOR, split_axis=0, concat_axis=0, tiled=True
    )
    loss, grad = gradient(
        logits, hit, jnp.swapaxes(stats, 0, 1), facts[1:2], facts[2:3]
    )
    return loss[0, :TOK], scattered_gradient(grad, mine, theirs)


def solution(mesh):
    mesh = Mesh(mesh.devices.reshape(SIZES), AXES)
    placed = (P(DP, None), P(TENSOR, DP), P(DP), P(), P(DP), P(DP))
    return jax.shard_map(
        shards, mesh=mesh, in_specs=placed, out_specs=(P(DP), P(TENSOR, DP)), check_vma=False
    )
```

time: 331 us -> 176 us (0.53)
  waiting for transfers between devices: 256 us -> 52.3 us
  starting transfers between devices: 0.08 us -> 65.5 us
  Pallas kernels: 0 us -> 44.9 us
  matrix products: 24.5 us -> 0 us
  blocking collectives: 33.9 us -> 9.75 us
  between operations: 14.1 us -> 0.96 us
    reduce_scatter x1 -> x0, waiting for transfers between devices: 166 us -> none  [shards(): lax.psum_scatter(lax.dot_general(columns, grad_logits, (((0,), (0,)), (()...]
    all_gather x1 -> x0, waiting for transfers between devices: 90 us -> none  [shards(): lax.all_gather(head, 'dp', axis=1, tiled=True)]
    ppermute x0 -> x28, starting transfers between devices: none -> 65.5 us  [move(): return lax.ppermute(value, axis, [(i, (i + by) % n) for i in range(n)])]
    ppermute x0 -> x28, waiting for transfers between devices: none -> 52.3 us  [move(): return lax.ppermute(value, axis, [(i, (i + by) % n) for i in range(n)])]
    pallas_call x0 -> x13, Pallas kernels: none -> 44.9 us  [the longest x5 25.2 us: block_call(): pl.pallas_call(body, out_shape=outs, in_specs=[pl.BlockSpec(memory_space=...]
    dot_general x2 -> x0, matrix products: 24.5 us -> none  [the longest x1 13.9 us: shards(): lax.dot_general(columns, grad_logits, (((0,), (0,)), ((), ())), preferred...]
    psum x1 -> x0, blocking collectives: 17.2 us -> none  [shards(): lax.psum((jnp.sum(jnp.exp(logits - row_max[:, None]), axis=1), target_pic...]
    pmax x1 -> x0, blocking collectives: 16.8 us -> none  [shards(): row_max = lax.pmax(local_max, 'tensor')]
  transfers between devices with their start and end apart: 2 -> 28, of which waited for: 2 -> 13; matrix products, arithmetic and copies ran while one was open for 0% -> 1% of each run, Pallas kernels for 0% -> 18%
where the time goes in v1:
time: 176 us; the launch traced here: 175 us
  starting transfers between devices  65.5 us (37%)
  waiting for transfers between devices  52.3 us (30%)
  Pallas kernels  44.9 us (26%)
  blocking collectives  9.75 us (6%)
  local copies, waits for them, and re-layouts  1.78 us (1%)
    ppermute x28, starting transfers between devices, move(): return lax.ppermute(value, axis, [(i, (i + by) % n) for i in range(n)])  65.5 us
    ppermute x28, waiting for transfers between devices, move(): return lax.ppermute(value, axis, [(i, (i + by) % n) for i in range(n)])  52.3 us
    pallas_call x5, Pallas kernels, block_call(): pl.pallas_call(body, out_shape=outs, in_specs=[pl.BlockSpec(memory_space=...  25.2 us
    pallas_call x3, Pallas kernels, pick(): pl.pallas_call(body, out_shape=jax.ShapeDtypeStruct((n, TOK, WIDE), BF16)...  17.2 us
    all_to_all x1, blocking collectives, shards(): lax.all_to_all(jnp.broadcast_to(stats[None], (8,) + stats.shape), TENSOR,...  9.75 us
  transfers between devices with their start and end apart: 28, of which 13 were waited for; matrix products, arithmetic and copies ran while one was open for 1% of the time, Pallas kernels for 18%

profile of v1, /device:TPU:8, one launch (start us, length us, event | category | flops | bytes accessed | tf_op | source)
XLA Modules:
  0.0 175.4 jit_solution(13861484659041049026)
XLA Ops:
  1.6 3.3 %collective-permute-start.1 = (bf16[192,512]{1,0:T(8,128)(2,1)S(1)}, bf16[192,512]{1,0:T(8,128)(2,1)S(1)}, u32[]{:S(2)}, u32[]{:S(2)}) collective-permute-start(bf16[192,512]{1,0:T(8,128)(2,1)S(1)} %slice.36), channel_id=1, source_target_pairs={{0,64},{64,128},{128,192},{192,0},{1,65},{65,129},{129,193},{193,1... | collective-permute-start | bytes 589832 | tf_op jit(solution)/shard_map/ppermute | solution.py:29
  5.0 4.9 %shard_map.78 = bf16[8,512,512]{2,1,0:T(8,128)(2,1)} custom-call(s32[8]{0:T(128)S(1)} %get-tuple-element.50.at_ref, bf16[512,16384]{1,0:T(8,128)(2,1)} %h_ref.5), custom_call_target="tpu_custom_call" | custom-call | bytes 25165824 | tf_op jit(solution)/shard_map/pallas_call | solution.py:71
  10.0 4.4 %collective-permute-done.1.refs_5_ = bf16[192,512]{1,0:T(8,128)(2,1)S(1)} collective-permute-done((bf16[192,512]{1,0:T(8,128)(2,1)S(1)}, bf16[192,512]{1,0:T(8,128)(2,1)S(1)}, u32[]{:S(2)}, u32[]{:S(2)}) %collective-permute-start.1) | collective-permute-done | bytes 196640 | tf_op jit(solution)/shard_map/ppermute | solution.py:29
  14.4 4.8 %shard_map.79 = bf16[8,512,512]{2,1,0:T(8,128)(2,1)} custom-call(s32[8]{0:T(128)S(1)} %get-tuple-element.24.at_ref, bf16[512,16384]{1,0:T(8,128)(2,1)} %h_ref.5), custom_call_target="tpu_custom_call" | custom-call | bytes 25165824 | tf_op jit(solution)/shard_map/pallas_call | solution.py:71
  19.3 5.4 %collective-permute-start.3 = (bf16[192,512]{1,0:T(8,128)(2,1)S(1)}, bf16[192,512]{1,0:T(8,128)(2,1)S(1)}, u32[]{:S(2)}, u32[]{:S(2)}) collective-permute-start(bf16[192,512]{1,0:T(8,128)(2,1)S(1)} %slice.36), channel_id=1, source_target_pairs={{0,192},{64,0},{128,64},{192,128},{1,193},{65,1},{129,65},{193,129... | collective-permute-start | bytes 589832 | tf_op jit(solution)/shard_map/ppermute | solution.py:29
  24.7 2.8 %collective-permute-start.6 = (bf16[256,512]{1,0:T(8,128)(2,1)S(1)}, bf16[256,512]{1,0:T(8,128)(2,1)S(1)}, u32[]{:S(2)}, u32[]{:S(2)}) collective-permute-start(bf16[256,512]{1,0:T(8,128)(2,1)S(1)} %copy-done.1), channel_id=1, source_target_pairs={{0,48},{16,0},{32,16},{48,32},{1,49},{17,1},{33,17},{49,33},{2,50}... | collective-permute-start | bytes 786440 | tf_op jit(solution)/shard_map/ppermute | solution.py:29
  27.5 6.2 %collective-permute-done.3.refs_4_ = bf16[192,512]{1,0:T(8,128)(2,1)S(1)} collective-permute-done((bf16[192,512]{1,0:T(8,128)(2,1)S(1)}, bf16[192,512]{1,0:T(8,128)(2,1)S(1)}, u32[]{:S(2)}, u32[]{:S(2)}) %collective-permute-start.3) | collective-permute-done | bytes 196640 | tf_op jit(solution)/shard_map/ppermute | solution.py:29
  33.7 3.0 %collective-permute-start.8 = (bf16[256,512]{1,0:T(8,128)(2,1)S(1)}, bf16[256,512]{1,0:T(8,128)(2,1)S(1)}, u32[]{:S(2)}, u32[]{:S(2)}) collective-permute-start(bf16[256,512]{1,0:T(8,128)(2,1)S(1)} %copy-done.1), channel_id=1, source_target_pairs={{0,32},{16,48},{32,0},{48,16},{1,33},{17,49},{33,1},{49,17},{2,34}... | collective-permute-start | bytes 786440 | tf_op jit(solution)/shard_map/ppermute | solution.py:29
  36.7 4.2 %collective-permute-start.4 = (bf16[192,512]{1,0:T(8,128)(2,1)S(1)}, bf16[192,512]{1,0:T(8,128)(2,1)S(1)}, u32[]{:S(2)}, u32[]{:S(2)}) collective-permute-start(bf16[192,512]{1,0:T(8,128)(2,1)S(1)} %slice.36), channel_id=1, source_target_pairs={{0,128},{64,192},{128,0},{192,64},{1,129},{65,193},{129,1},{193,65... | collective-permute-start | bytes 589832 | tf_op jit(solution)/shard_map/ppermute | solution.py:29
  43.2 4.7 %collective-permute-start.12 = (bf16[256,512]{1,0:T(8,128)(2,1)S(1)}, bf16[256,512]{1,0:T(8,128)(2,1)S(1)}, u32[]{:S(2)}, u32[]{:S(2)}) collective-permute-start(bf16[256,512]{1,0:T(8,128)(2,1)S(1)} %pad_maximum_fusion), channel_id=1, source_target_pairs={{0,192},{64,0},{128,64},{192,128},{1,193},{65,1},{129,65},{193,129... | collective-permute-start | bytes 786440 | tf_op jit(solution)/shard_map/ppermute | solution.py:29
  47.9 2.8 %collective-permute-start.10 = (bf16[576,512]{1,0:T(8,128)(2,1)S(1)}, bf16[576,512]{1,0:T(8,128)(2,1)S(1)}, u32[]{:S(2)}, u32[]{:S(2)}) collective-permute-start(bf16[576,512]{1,0:T(8,128)(2,1)S(1)} %constant_dynamic-update-slice_fusion), channel_id=1, source_target_pairs={{0,48},{16,0},{32,16},{48,32},{1,49},{17,1},{33,17},{49,33},{2,50}... | collective-permute-start | bytes 1769480 | tf_op jit(solution)/shard_map/ppermute | solution.py:29
  50.7 8.7 %collective-permute-done.12.refs_2_ = bf16[256,512]{1,0:T(8,128)(2,1)S(1)} collective-permute-done((bf16[256,512]{1,0:T(8,128)(2,1)S(1)}, bf16[256,512]{1,0:T(8,128)(2,1)S(1)}, u32[]{:S(2)}, u32[]{:S(2)}) %collective-permute-start.12) | collective-permute-done | bytes 262176 | tf_op jit(solution)/shard_map/ppermute | solution.py:29
  62.2 7.5 %shard_map.77.m_ref = bf16[16,512,512]{2,1,0:T(8,128)(2,1)} custom-call(s32[16]{0:T(128)S(1)} %broadcast_add_fusion.1.at_ref, bf16[512,16384]{1,0:T(8,128)(2,1)} %h_ref.5), custom_call_target="tpu_custom_call" | custom-call | bytes 50331648 | tf_op jit(solution)/shard_map/pallas_call | solution.py:71
  69.7 3.6 %collective-permute-start.9 = (bf16[256,512]{1,0:T(8,128)(2,1)S(1)}, bf16[256,512]{1,0:T(8,128)(2,1)S(1)}, u32[]{:S(2)}, u32[]{:S(2)}) collective-permute-start(bf16[256,512]{1,0:T(8,128)(2,1)S(1)} %pad_maximum_fusion), channel_id=1, source_target_pairs={{0,128},{64,192},{128,0},{192,64},{1,129},{65,193},{129,1},{193,65... | collective-permute-start | bytes 786440 | tf_op jit(solution)/shard_map/ppermute | solution.py:29
  73.3 4.1 %shard_map.80.refs_4_ = f32[256,1024]{1,0:T(8,128)S(1)} custom-call(bf16[16,512,512]{2,1,0:T(8,128)(2,1)} %shard_map.77.m_ref, bf16[8,512,512]{2,1,0:T(8,128)(2,1)} %copy-done.2, bf16[8,512,512]{2,1,0:T(8,128)(2,1)} %collective-permute-done.2.t1_ref, bf16[256,512]{1,0:T(8,128)(2,1)S(1)} %copy-done.1, bf16[256,512]{1,0:T(8,128)(2,1)S(1)} %collective-permute-done.6.refs_1_, ...), custom_call_target="tpu_custom_call" | custom-call | flops 1677721600 | bytes 7340032 | tf_op jit(solution)/shard_map/pallas_call | solution.py:105
  78.2 6.3 %shard_map.81.refs_2_ = f32[256,1024]{1,0:T(8,128)S(1)} custom-call(bf16[16,512,512]{2,1,0:T(8,128)(2,1)} %shard_map.77.m_ref, bf16[8,512,512]{2,1,0:T(8,128)(2,1)} %copy-done.2, bf16[8,512,512]{2,1,0:T(8,128)(2,1)} %collective-permute-done.2.t1_ref, bf16[576,512]{1,0:T(8,128)(2,1)S(1)} %collective-permute-done.10.refs_0_, ...), custom_call_target="tpu_custom_call" | custom-call | flops 1744830464 | bytes 10485760 | tf_op jit(solution)/shard_map/pallas_call | solution.py:105
  84.5 2.3 %collective-permute-done.9.refs_1_ = bf16[256,512]{1,0:T(8,128)(2,1)S(1)} collective-permute-done((bf16[256,512]{1,0:T(8,128)(2,1)S(1)}, bf16[256,512]{1,0:T(8,128)(2,1)S(1)}, u32[]{:S(2)}, u32[]{:S(2)}) %collective-permute-start.9) | collective-permute-done | bytes 262176 | tf_op jit(solution)/shard_map/ppermute | solution.py:29
  86.9 4.0 %shard_map.82.mine = f32[256,1024]{1,0:T(8,128)S(1)} custom-call(bf16[16,512,512]{2,1,0:T(8,128)(2,1)} %shard_map.77.m_ref, bf16[8,512,512]{2,1,0:T(8,128)(2,1)} %copy-done.2, bf16[8,512,512]{2,1,0:T(8,128)(2,1)} %collective-permute-done.2.t1_ref, bf16[576,512]{1,0:T(8,128)(2,1)S(1)} %collective-permute-done.5.refs_0_, ...), custom_call_target="tpu_custom_call" | custom-call | flops 872415232 | bytes 6291456 | tf_op jit(solution)/shard_map/pallas_call | solution.py:105
  94.5 9.8 %all_to_all.5 = f32[8,3,1024]{2,1,0:T(4,128)S(1)} all-to-all(f32[8,3,1024]{2,1,0:T(4,128)S(1)} %broadcast_in_dim.2), channel_id=1, replica_groups=mesh['zh'=4,'x'=4,'c'=2,'zl'=2,'y'=4] {'zl','y'}, dimensions={0} | all-to-all | bytes 196608 | tf_op jit(solution)/shard_map/all_to_all | solution.py:311
  104.6 7.7 %shard_map.86 = (bf16[576,512]{1,0:T(8,128)(2,1)S(1)}, bf16[576,512]{1,0:T(8,128)(2,1)S(1)}, bf16[576,512]{1,0:T(8,128)(2,1)S(1)}, f32[576,512]{1,0:T(8,128)}, b...) custom-call(bf16[16,512,512]{2,1,0:T(8,128)(2,1)} %shard_map.77.m_ref, ...), custom_call_target="tpu_custom_call" | custom-call | flops 3221225472 | bytes 12582912 | tf_op jit(solution)/shard_map/pallas_call | solution.py:105
  112.4 3.3 %collective-permute-start.16 = (bf16[256,512]{1,0:T(8,128)(2,1)S(1)}, bf16[256,512]{1,0:T(8,128)(2,1)S(1)}, u32[]{:S(2)}, u32[]{:S(2)}) collective-permute-start(bf16[256,512]{1,0:T(8,128)(2,1)S(1)} %get-tuple-element.32), channel_id=1, source_target_pairs={{0,64},{64,128},{128,192},{192,0},{1,65},{65,129},{129,193},{193,1... | collective-permute-start | bytes 786440 | tf_op jit(solution)/shard_map/ppermute | solution.py:29
  118.9 4.3 %collective-permute-start.17 = (bf16[256,512]{1,0:T(8,128)(2,1)S(1)}, bf16[256,512]{1,0:T(8,128)(2,1)S(1)}, u32[]{:S(2)}, u32[]{:S(2)}) collective-permute-start(bf16[256,512]{1,0:T(8,128)(2,1)S(1)} %get-tuple-element.33), channel_id=1, source_target_pairs={{0,128},{64,192},{128,0},{192,64},{1,129},{65,193},{129,1},{193,65... | collective-permute-start | bytes 786440 | tf_op jit(solution)/shard_map/ppermute | solution.py:29
  123.3 3.4 %collective-permute-done.16.one = bf16[256,512]{1,0:T(8,128)(2,1)S(1)} collective-permute-done((bf16[256,512]{1,0:T(8,128)(2,1)S(1)}, bf16[256,512]{1,0:T(8,128)(2,1)S(1)}, u32[]{:S(2)}, u32[]{:S(2)}) %collective-permute-start.16) | collective-permute-done | bytes 262176 | tf_op jit(solution)/shard_map/ppermute | solution.py:29
  126.6 7.0 %collective-permute-start.18 = (bf16[256,512]{1,0:T(8,128)(2,1)S(1)}, bf16[256,512]{1,0:T(8,128)(2,1)S(1)}, u32[]{:S(2)}, u32[]{:S(2)}) collective-permute-start(bf16[256,512]{1,0:T(8,128)(2,1)S(1)} %get-tuple-element.34), channel_id=1, source_target_pairs={{0,192},{64,0},{128,64},{192,128},{1,193},{65,1},{129,65},{193,129... | collective-permute-start | bytes 786440 | tf_op jit(solution)/shard_map/ppermute | solution.py:29
  133.6 3.0 %shard_map.85 = (f32[768,512]{1,0:T(8,128)S(1)}, f32[256,512]{1,0:T(8,128)S(1)}) custom-call(bf16[16,512,512]{2,1,0:T(8,128)(2,1)} %shard_map.77.m_ref, bf16[8,512,512]{2,1,0:T(8,128)(2,1)} %copy-done.2, bf16[8,512,512]{2,1,0:T(8,128)(2,1)} %collective-permute-done.2.t1_ref, bf16[256,1024]{1,0:T(8,128)(2,1)S(1)} %get-tuple-element.29.refs_0_), custom_call_target="tpu_custom_call" | custom-call | flops 1073741824 | bytes 4194304 | tf_op jit(solution)/shard_map/pallas_call | solution.py:105
  136.6 4.7 %collective-permute-done.17.two = bf16[256,512]{1,0:T(8,128)(2,1)S(1)} collective-permute-done((bf16[256,512]{1,0:T(8,128)(2,1)S(1)}, bf16[256,512]{1,0:T(8,128)(2,1)S(1)}, u32[]{:S(2)}, u32[]{:S(2)}) %collective-permute-start.17) | collective-permute-done | bytes 262176 | tf_op jit(solution)/shard_map/ppermute | solution.py:29
  141.6 4.5 %collective-permute-start.19 = (bf16[256,512]{1,0:T(8,128)(2,1)S(1)}, bf16[256,512]{1,0:T(8,128)(2,1)S(1)}, u32[]{:S(2)}, u32[]{:S(2)}) collective-permute-start(bf16[256,512]{1,0:T(8,128)(2,1)S(1)} %get-tuple-element.36), channel_id=1, source_target_pairs={{0,16},{16,32},{32,48},{48,0},{1,17},{17,33},{33,49},{49,1},{2,18}... | collective-permute-start | bytes 786440 | tf_op jit(solution)/shard_map/ppermute | solution.py:29
  146.3 2.5 %collective-permute-start.21 = (bf16[256,512]{1,0:T(8,128)(2,1)S(1)}, bf16[256,512]{1,0:T(8,128)(2,1)S(1)}, u32[]{:S(2)}, u32[]{:S(2)}) collective-permute-start(bf16[256,512]{1,0:T(8,128)(2,1)S(1)} %get-tuple-element.38), channel_id=1, source_target_pairs={{0,48},{16,0},{32,16},{48,32},{1,49},{17,1},{33,17},{49,33},{2,50}... | collective-permute-start | bytes 786440 | tf_op jit(solution)/shard_map/ppermute | solution.py:29
  149.1 2.4 %collective-permute-start.25 = (bf16[192,512]{1,0:T(8,128)(2,1)S(1)}, bf16[192,512]{1,0:T(8,128)(2,1)S(1)}, u32[]{:S(2)}, u32[]{:S(2)}) collective-permute-start(bf16[192,512]{1,0:T(8,128)(2,1)S(1)} %get-tuple-element.43), channel_id=1, source_target_pairs={{0,64},{64,128},{128,192},{192,0},{1,65},{65,129},{129,193},{193,1... | collective-permute-start | bytes 589832 | tf_op jit(solution)/shard_map/ppermute | solution.py:29
  151.5 4.6 %collective-permute-start.26 = (bf16[192,512]{1,0:T(8,128)(2,1)S(1)}, bf16[192,512]{1,0:T(8,128)(2,1)S(1)}, u32[]{:S(2)}, u32[]{:S(2)}) collective-permute-start(bf16[192,512]{1,0:T(8,128)(2,1)S(1)} %get-tuple-element.44), channel_id=1, source_target_pairs={{0,128},{64,192},{128,0},{192,64},{1,129},{65,193},{129,1},{193,65... | collective-permute-start | bytes 589832 | tf_op jit(solution)/shard_map/ppermute | solution.py:29
  157.3 6.7 %collective-permute-done.25.z1 = bf16[192,512]{1,0:T(8,128)(2,1)S(1)} collective-permute-done((bf16[192,512]{1,0:T(8,128)(2,1)S(1)}, bf16[192,512]{1,0:T(8,128)(2,1)S(1)}, u32[]{:S(2)}, u32[]{:S(2)}) %collective-permute-start.25) | collective-permute-done | bytes 196640 | tf_op jit(solution)/shard_map/ppermute | solution.py:29
  165.8 8.5 %collective-permute-done.27.z3 = bf16[192,512]{1,0:T(8,128)(2,1)S(1)} collective-permute-done((bf16[192,512]{1,0:T(8,128)(2,1)S(1)}, bf16[192,512]{1,0:T(8,128)(2,1)S(1)}, u32[]{:S(2)}, u32[]{:S(2)}) %collective-permute-start.27) | collective-permute-done | bytes 196640 | tf_op jit(solution)/shard_map/ppermute | solution.py:29
  (74 shorter events, 18.8 us)
Async XLA Ops:
  1.6 12.8 %collective-permute-start.1 = (bf16[192,512]{1,0:T(8,128)(2,1)S(1)}, bf16[192,512]{1,0:T(8,128)(2,1)S(1)}, u32[]{:S(2)}, u32[]{:S(2)}) collective-permute-start(bf16[192,512]{1,0:T(8,128)(2,1)S(1)} %slice.36), channel_id=1, source_target_pairs={{0,64},{64,128},{128,192},{192,0},{1,65},{65,129},{129,193},{193,1... | collective-permute-start | bytes 589832 | tf_op jit(solution)/shard_map/ppermute | solution.py:29
  9.9 50.2 %collective-permute-start = (bf16[8,512,512]{2,1,0:T(8,128)(2,1)}, bf16[8,512,512]{2,1,0:T(8,128)(2,1)S(1)}, u32[]{:S(2)}, u32[]{:S(2)}) collective-permute-start(bf16[8,512,512]{2,1,0:T(8,128)(2,1)} %shard_map.78), channel_id=1, source_target_pairs={{0,8},{8,0},{1,9},{9,1},{2,10},{10,2},{3,11},{11,3},{4,12},{12,4},... | collective-permute-start | bytes 12582920 | tf_op jit(solution)/shard_map/ppermute | solution.py:29
  14.4 10.3 %copy-start.1 = (bf16[256,512]{1,0:T(8,128)(2,1)S(1)}, bf16[256,512]{1,0:T(8,128)(2,1)}, u32[]{:S(2)}) copy-start(bf16[256,512]{1,0:T(8,128)(2,1)} %refs_0_.1) | copy-start | bytes 786436
  19.2 50.5 %collective-permute-start.2 = (bf16[8,512,512]{2,1,0:T(8,128)(2,1)}, bf16[8,512,512]{2,1,0:T(8,128)(2,1)}, u32[]{:S(2)}, u32[]{:S(2)}) collective-permute-start(bf16[8,512,512]{2,1,0:T(8,128)(2,1)} %shard_map.79), channel_id=1, source_target_pairs={{0,8},{8,0},{1,9},{9,1},{2,10},{10,2},{3,11},{11,3},{4,12},{12,4},... | collective-permute-start | bytes 12582920 | tf_op jit(solution)/shard_map/ppermute | solution.py:29
  19.3 14.4 %collective-permute-start.3 = (bf16[192,512]{1,0:T(8,128)(2,1)S(1)}, bf16[192,512]{1,0:T(8,128)(2,1)S(1)}, u32[]{:S(2)}, u32[]{:S(2)}) collective-permute-start(bf16[192,512]{1,0:T(8,128)(2,1)S(1)} %slice.36), channel_id=1, source_target_pairs={{0,192},{64,0},{128,64},{192,128},{1,193},{65,1},{129,65},{193,129... | collective-permute-start | bytes 589832 | tf_op jit(solution)/shard_map/ppermute | solution.py:29
  24.7 12.0 %collective-permute-start.6 = (bf16[256,512]{1,0:T(8,128)(2,1)S(1)}, bf16[256,512]{1,0:T(8,128)(2,1)S(1)}, u32[]{:S(2)}, u32[]{:S(2)}) collective-permute-start(bf16[256,512]{1,0:T(8,128)(2,1)S(1)} %copy-done.1), channel_id=1, source_target_pairs={{0,48},{16,0},{32,16},{48,32},{1,49},{17,1},{33,17},{49,33},{2,50}... | collective-permute-start | bytes 786440 | tf_op jit(solution)/shard_map/ppermute | solution.py:29
  27.5 13.5 %collective-permute-start.7 = (bf16[256,512]{1,0:T(8,128)(2,1)S(1)}, bf16[256,512]{1,0:T(8,128)(2,1)S(1)}, u32[]{:S(2)}, u32[]{:S(2)}) collective-permute-start(bf16[256,512]{1,0:T(8,128)(2,1)S(1)} %copy-done.1), channel_id=1, source_target_pairs={{0,16},{16,32},{32,48},{48,0},{1,17},{17,33},{33,49},{49,1},{2,18}... | collective-permute-start | bytes 786440 | tf_op jit(solution)/shard_map/ppermute | solution.py:29
  33.7 9.5 %collective-permute-start.8 = (bf16[256,512]{1,0:T(8,128)(2,1)S(1)}, bf16[256,512]{1,0:T(8,128)(2,1)S(1)}, u32[]{:S(2)}, u32[]{:S(2)}) collective-permute-start(bf16[256,512]{1,0:T(8,128)(2,1)S(1)} %copy-done.1), channel_id=1, source_target_pairs={{0,32},{16,48},{32,0},{48,16},{1,33},{17,49},{33,1},{49,17},{2,34}... | collective-permute-start | bytes 786440 | tf_op jit(solution)/shard_map/ppermute | solution.py:29
  36.7 11.1 %collective-permute-start.4 = (bf16[192,512]{1,0:T(8,128)(2,1)S(1)}, bf16[192,512]{1,0:T(8,128)(2,1)S(1)}, u32[]{:S(2)}, u32[]{:S(2)}) collective-permute-start(bf16[192,512]{1,0:T(8,128)(2,1)S(1)} %slice.36), channel_id=1, source_target_pairs={{0,128},{64,192},{128,0},{192,64},{1,129},{65,193},{129,1},{193,65... | collective-permute-start | bytes 589832 | tf_op jit(solution)/shard_map/ppermute | solution.py:29
  43.2 16.3 %collective-permute-start.12 = (bf16[256,512]{1,0:T(8,128)(2,1)S(1)}, bf16[256,512]{1,0:T(8,128)(2,1)S(1)}, u32[]{:S(2)}, u32[]{:S(2)}) collective-permute-start(bf16[256,512]{1,0:T(8,128)(2,1)S(1)} %pad_maximum_fusion), channel_id=1, source_target_pairs={{0,192},{64,0},{128,64},{192,128},{1,193},{65,1},{129,65},{193,129... | collective-permute-start | bytes 786440 | tf_op jit(solution)/shard_map/ppermute | solution.py:29
  47.9 29.6 %collective-permute-start.10 = (bf16[576,512]{1,0:T(8,128)(2,1)S(1)}, bf16[576,512]{1,0:T(8,128)(2,1)S(1)}, u32[]{:S(2)}, u32[]{:S(2)}) collective-permute-start(bf16[576,512]{1,0:T(8,128)(2,1)S(1)} %constant_dynamic-update-slice_fusion), channel_id=1, source_target_pairs={{0,48},{16,0},{32,16},{48,32},{1,49},{17,1},{33,17},{49,33},{2,50}... | collective-permute-start | bytes 1769480 | tf_op jit(solution)/shard_map/ppermute | solution.py:29
  50.7 27.4 %collective-permute-start.11 = (bf16[576,512]{1,0:T(8,128)(2,1)S(1)}, bf16[576,512]{1,0:T(8,128)(2,1)S(1)}, u32[]{:S(2)}, u32[]{:S(2)}) collective-permute-start(bf16[576,512]{1,0:T(8,128)(2,1)S(1)} %constant_dynamic-update-slice_fusion), channel_id=1, source_target_pairs={{0,16},{16,32},{32,48},{48,0},{1,17},{17,33},{33,49},{49,1},{2,18}... | collective-permute-start | bytes 1769480 | tf_op jit(solution)/shard_map/ppermute | solution.py:29
  59.5 27.4 %collective-permute-start.5 = (bf16[576,512]{1,0:T(8,128)(2,1)S(1)}, bf16[576,512]{1,0:T(8,128)(2,1)S(1)}, u32[]{:S(2)}, u32[]{:S(2)}) collective-permute-start(bf16[576,512]{1,0:T(8,128)(2,1)S(1)} %constant_dynamic-update-slice_fusion), channel_id=1, source_target_pairs={{0,32},{16,48},{32,0},{48,16},{1,33},{17,49},{33,1},{49,17},{2,34}... | collective-permute-start | bytes 1769480 | tf_op jit(solution)/shard_map/ppermute | solution.py:29
  60.2 9.5 %copy-start.2 = (bf16[8,512,512]{2,1,0:T(8,128)(2,1)}, bf16[8,512,512]{2,1,0:T(8,128)(2,1)S(1)}, u32[]{:S(2)}) copy-start(bf16[8,512,512]{2,1,0:T(8,128)(2,1)S(1)} %collective-permute-done.t0_ref) | copy-start | bytes 12582916
  60.2 17.3 %collective-permute-start.13 = (bf16[256,512]{1,0:T(8,128)(2,1)S(1)}, bf16[256,512]{1,0:T(8,128)(2,1)S(1)}, u32[]{:S(2)}, u32[]{:S(2)}) collective-permute-start(bf16[256,512]{1,0:T(8,128)(2,1)S(1)} %pad_maximum_fusion), channel_id=1, source_target_pairs={{0,64},{64,128},{128,192},{192,0},{1,65},{65,129},{129,193},{193,1... | collective-permute-start | bytes 786440 | tf_op jit(solution)/shard_map/ppermute | solution.py:29
  69.7 17.2 %collective-permute-start.9 = (bf16[256,512]{1,0:T(8,128)(2,1)S(1)}, bf16[256,512]{1,0:T(8,128)(2,1)S(1)}, u32[]{:S(2)}, u32[]{:S(2)}) collective-permute-start(bf16[256,512]{1,0:T(8,128)(2,1)S(1)} %pad_maximum_fusion), channel_id=1, source_target_pairs={{0,128},{64,192},{128,0},{192,64},{1,129},{65,193},{129,1},{193,65... | collective-permute-start | bytes 786440 | tf_op jit(solution)/shard_map/ppermute | solution.py:29
  84.5 7.1 %copy-start.6 = (s32[2]{0:T(128)S(1)}, s32[2]{0:T(128)}, u32[]{:S(2)}) copy-start(s32[2]{0:T(128)} %param.9) | copy-start | bytes 28
  90.9 2.9 %collective-permute-start.14 = (f32[256,1024]{1,0:T(8,128)S(1)}, f32[256,1024]{1,0:T(8,128)S(1)}, u32[]{:S(2)}, u32[]{:S(2)}) collective-permute-start(f32[256,1024]{1,0:T(8,128)S(1)} %shard_map.82.mine), channel_id=1, source_target_pairs={{0,8},{8,0},{1,9},{9,1},{2,10},{10,2},{3,11},{11,3},{4,12},{12,4},... | collective-permute-start | bytes 3145736 | tf_op jit(solution)/shard_map/ppermute | solution.py:29
  91.0 2.6 %collective-permute-start.15 = (f32[3,512]{1,0:T(4,128)S(1)}, f32[3,512]{1,0:T(4,128)S(1)}, u32[]{:S(2)}, u32[]{:S(2)}) collective-permute-start(f32[3,512]{1,0:T(4,128)S(1)} %pad_maximum_fusion.1), channel_id=1, source_target_pairs={{0,8},{8,0},{1,9},{9,1},{2,10},{10,2},{3,11},{11,3},{4,12},{12,4},... | collective-permute-start | bytes 18440 | tf_op jit(solution)/shard_map/ppermute | solution.py:29
  112.4 14.3 %collective-permute-start.16 = (bf16[256,512]{1,0:T(8,128)(2,1)S(1)}, bf16[256,512]{1,0:T(8,128)(2,1)S(1)}, u32[]{:S(2)}, u32[]{:S(2)}) collective-permute-start(bf16[256,512]{1,0:T(8,128)(2,1)S(1)} %get-tuple-element.32), channel_id=1, source_target_pairs={{0,64},{64,128},{128,192},{192,0},{1,65},{65,129},{129,193},{193,1... | collective-permute-start | bytes 786440 | tf_op jit(solution)/shard_map/ppermute | solution.py:29
  115.7 30.6 %collective-permute-start.22 = (bf16[576,512]{1,0:T(8,128)(2,1)S(1)}, bf16[576,512]{1,0:T(8,128)(2,1)S(1)}, u32[]{:S(2)}, u32[]{:S(2)}) collective-permute-start(bf16[576,512]{1,0:T(8,128)(2,1)S(1)} %get-tuple-element.40), channel_id=1, source_target_pairs={{0,16},{16,32},{32,48},{48,0},{1,17},{17,33},{33,49},{49,1},{2,18}... | collective-permute-start | bytes 1769480 | tf_op jit(solution)/shard_map/ppermute | solution.py:29
  115.7 33.2 %collective-permute-start.23 = (bf16[576,512]{1,0:T(8,128)(2,1)S(1)}, bf16[576,512]{1,0:T(8,128)(2,1)S(1)}, u32[]{:S(2)}, u32[]{:S(2)}) collective-permute-start(bf16[576,512]{1,0:T(8,128)(2,1)S(1)} %get-tuple-element.41), channel_id=1, source_target_pairs={{0,32},{16,48},{32,0},{48,16},{1,33},{17,49},{33,1},{49,17},{2,34}... | collective-permute-start | bytes 1769480 | tf_op jit(solution)/shard_map/ppermute | solution.py:29
  116.7 32.2 %collective-permute-start.24 = (bf16[576,512]{1,0:T(8,128)(2,1)S(1)}, bf16[576,512]{1,0:T(8,128)(2,1)S(1)}, u32[]{:S(2)}, u32[]{:S(2)}) collective-permute-start(bf16[576,512]{1,0:T(8,128)(2,1)S(1)} %get-tuple-element.42), channel_id=1, source_target_pairs={{0,48},{16,0},{32,16},{48,32},{1,49},{17,1},{33,17},{49,33},{2,50}... | collective-permute-start | bytes 1769480 | tf_op jit(solution)/shard_map/ppermute | solution.py:29
  118.9 22.5 %collective-permute-start.17 = (bf16[256,512]{1,0:T(8,128)(2,1)S(1)}, bf16[256,512]{1,0:T(8,128)(2,1)S(1)}, u32[]{:S(2)}, u32[]{:S(2)}) collective-permute-start(bf16[256,512]{1,0:T(8,128)(2,1)S(1)} %get-tuple-element.33), channel_id=1, source_target_pairs={{0,128},{64,192},{128,0},{192,64},{1,129},{65,193},{129,1},{193,65... | collective-permute-start | bytes 786440 | tf_op jit(solution)/shard_map/ppermute | solution.py:29
  126.6 22.2 %copy-start = (f32[576,512]{1,0:T(8,128)S(1)}, f32[576,512]{1,0:T(8,128)}, u32[]{:S(2)}) copy-start(f32[576,512]{1,0:T(8,128)} %get-tuple-element.39.kept) | copy-start | bytes 3538948
  126.6 14.7 %collective-permute-start.18 = (bf16[256,512]{1,0:T(8,128)(2,1)S(1)}, bf16[256,512]{1,0:T(8,128)(2,1)S(1)}, u32[]{:S(2)}, u32[]{:S(2)}) collective-permute-start(bf16[256,512]{1,0:T(8,128)(2,1)S(1)} %get-tuple-element.34), channel_id=1, source_target_pairs={{0,192},{64,0},{128,64},{192,128},{1,193},{65,1},{129,65},{193,129... | collective-permute-start | bytes 786440 | tf_op jit(solution)/shard_map/ppermute | solution.py:29
  141.6 14.5 %collective-permute-start.19 = (bf16[256,512]{1,0:T(8,128)(2,1)S(1)}, bf16[256,512]{1,0:T(8,128)(2,1)S(1)}, u32[]{:S(2)}, u32[]{:S(2)}) collective-permute-start(bf16[256,512]{1,0:T(8,128)(2,1)S(1)} %get-tuple-element.36), channel_id=1, source_target_pairs={{0,16},{16,32},{32,48},{48,0},{1,17},{17,33},{33,49},{49,1},{2,18}... | collective-permute-start | bytes 786440 | tf_op jit(solution)/shard_map/ppermute | solution.py:29
  146.0 11.3 %collective-permute-start.20 = (bf16[256,512]{1,0:T(8,128)(2,1)S(1)}, bf16[256,512]{1,0:T(8,128)(2,1)S(1)}, u32[]{:S(2)}, u32[]{:S(2)}) collective-permute-start(bf16[256,512]{1,0:T(8,128)(2,1)S(1)} %get-tuple-element.37), channel_id=1, source_target_pairs={{0,32},{16,48},{32,0},{48,16},{1,33},{17,49},{33,1},{49,17},{2,34}... | collective-permute-start | bytes 786440 | tf_op jit(solution)/shard_map/ppermute | solution.py:29
  146.3 11.0 %collective-permute-start.21 = (bf16[256,512]{1,0:T(8,128)(2,1)S(1)}, bf16[256,512]{1,0:T(8,128)(2,1)S(1)}, u32[]{:S(2)}, u32[]{:S(2)}) collective-permute-start(bf16[256,512]{1,0:T(8,128)(2,1)S(1)} %get-tuple-element.38), channel_id=1, source_target_pairs={{0,48},{16,0},{32,16},{48,32},{1,49},{17,1},{33,17},{49,33},{2,50}... | collective-permute-start | bytes 786440 | tf_op jit(solution)/shard_map/ppermute | solution.py:29
  149.1 14.9 %collective-permute-start.25 = (bf16[192,512]{1,0:T(8,128)(2,1)S(1)}, bf16[192,512]{1,0:T(8,128)(2,1)S(1)}, u32[]{:S(2)}, u32[]{:S(2)}) collective-permute-start(bf16[192,512]{1,0:T(8,128)(2,1)S(1)} %get-tuple-element.43), channel_id=1, source_target_pairs={{0,64},{64,128},{128,192},{192,0},{1,65},{65,129},{129,193},{193,1... | collective-permute-start | bytes 589832 | tf_op jit(solution)/shard_map/ppermute | solution.py:29
  151.5 14.3 %collective-permute-start.26 = (bf16[192,512]{1,0:T(8,128)(2,1)S(1)}, bf16[192,512]{1,0:T(8,128)(2,1)S(1)}, u32[]{:S(2)}, u32[]{:S(2)}) collective-permute-start(bf16[192,512]{1,0:T(8,128)(2,1)S(1)} %get-tuple-element.44), channel_id=1, source_target_pairs={{0,128},{64,192},{128,0},{192,64},{1,129},{65,193},{129,1},{193,65... | collective-permute-start | bytes 589832 | tf_op jit(solution)/shard_map/ppermute | solution.py:29
  156.1 18.2 %collective-permute-start.27 = (bf16[192,512]{1,0:T(8,128)(2,1)S(1)}, bf16[192,512]{1,0:T(8,128)(2,1)S(1)}, u32[]{:S(2)}, u32[]{:S(2)}) collective-permute-start(bf16[192,512]{1,0:T(8,128)(2,1)S(1)} %get-tuple-element.45), channel_id=1, source_target_pairs={{0,192},{64,0},{128,64},{192,128},{1,193},{65,1},{129,65},{193,129... | collective-permute-start | bytes 589832 | tf_op jit(solution)/shard_map/ppermute | solution.py:29
  (3 other events, 19.6 us)
